TPU v7x, 512 devices: a whole 4x4x16 slice. The times are simulated.
512 devices in a mesh: dp: 16 (over y, x_lo, core), ctx: 32 (over x_hi, z).
Axes of the slice: x: 4 (x_hi: 2, x_lo: 2; x = x_hi * 2 + x_lo), y: 4, z: 16, core: 2. Of those that a mesh axis runs over, the one named last changes fastest.
Arguments:
- grad_out: bfloat16 [16, 4096, 512], P('dp', 'ctx'), may hold values from -6 to 6
- query_proj: bfloat16 [16, 4096, 512], P('dp', 'ctx'), may hold values from -6 to 6
- key_proj: bfloat16 [16, 4096, 512], P('dp', 'ctx'), may hold values from -6 to 6
- value_proj: bfloat16 [16, 4096, 512], P('dp', 'ctx'), may hold values from -6 to 6
- filters: bfloat16 [512, 4096], P(('ctx', 'dp')), may hold values from -1 to 1
Outputs:
- grad_query: bfloat16 [16, 4096, 512], P('dp', 'ctx')
- grad_key: bfloat16 [16, 4096, 512], P('dp', 'ctx')
- grad_value: bfloat16 [16, 4096, 512], P('dp', 'ctx')
- grad_filters: float32 [512, 4096], P(('ctx', 'dp'))
All inputs are finite; a program needn't handle non-finite values.
Results may differ from a plain program's by a relative error of at most 0.022.
Values may be sent and summed in bfloat16 or wider, within the bound.
A program may use at most 64 MiB of HBM per device.

v0:
```python
import functools
import math

import jax
import jax.numpy as jnp
import ml_dtypes
import numpy as np
from jax import lax
from jax.experimental import pallas as pl
from jax.experimental.pallas import tpu as pltpu
from jax.sharding import PartitionSpec as P

MESH = pl.DeviceIdType.MESH
BF16 = ml_dtypes.bfloat16
HALF = 8


def split_table(table):
    high = table.astype(np.float32).astype(BF16)
    low = (table - high.astype(np.float64)).astype(np.float32).astype(BF16)
    return high, low


def make_tables(blocks, width):
    points = blocks * width
    freq = np.arange(blocks) + 0.25
    eye = np.eye(HALF)
    angle_one = 2.0 * np.pi * freq[:, None] * np.arange(blocks)[None, :] / blocks
    cos_one, sin_one = np.cos(angle_one), np.sin(angle_one)

    def spread(block, rows, cols):
        out = block[:, None, :, None] * eye[None, :, None, :]
        if rows == "ck":
            out = out.transpose(1, 0, 2, 3)
        if cols == "ck":
            out = out.transpose(0, 1, 3, 2)
        n = blocks * HALF
        return out.reshape(n, n)

    def first(cols):
        high, low = split_table(
            np.concatenate([spread(cos_one, "kc", cols), spread(-sin_one, "kc", cols)], 0)
        )
        return np.concatenate([high, low], 1)

    def last(rows):
        return split_table(
            np.concatenate([spread(cos_one.T, rows, "kc"), spread(-sin_one.T, rows, "kc")], 1)
            / points
        )

    angle_two = 2.0 * np.pi * (np.arange(width)[:, None] * np.arange(width)[None, :] % width) / width
    cos_two, sin_two = np.cos(angle_two), np.sin(angle_two)
    fwd_high, fwd_low = split_table(np.block([[cos_two, -sin_two], [sin_two, cos_two]]))
    inv_high, inv_low = split_table(np.block([[cos_two, sin_two], [-sin_two, cos_two]]))
    angle_twist = 2.0 * np.pi * freq[:, None] * np.arange(width)[None, :] / points
    twist = np.stack([np.cos(angle_twist), np.sin(angle_twist)])
    twist = np.repeat(twist, HALF, axis=1).astype(np.float32)
    last_tok, last_lag = last("kc"), last("ck")
    return (
        first("kc"),
        first("ck"),
        np.concatenate([fwd_high, fwd_high, fwd_low], 0),
        np.concatenate([inv_high, inv_high, inv_low], 0),
        np.concatenate([last_tok[0], last_tok[0], last_tok[1]], 1),
        np.concatenate([last_lag[0], last_lag[0], last_lag[1]], 1),
        twist,
    )


def dot(a, b):
    return jnp.dot(a, b, preferred_element_type=jnp.float32)


def split(x):
    high = x.astype(jnp.bfloat16)
    low = (x - high.astype(jnp.float32)).astype(jnp.bfloat16)
    return high, low


def forward(signal, first, second, twist):
    n, width = signal.shape[0], signal.shape[1] // 2
    part = dot(first, jnp.concatenate([signal, signal], 0))
    out = []
    for half in range(2):
        lanes = slice(half * width, (half + 1) * width)
        re, im = part[:n, lanes], part[n:, lanes]
        turned = jnp.concatenate(
            [re * twist[0] + im * twist[1], im * twist[0] - re * twist[1]], 1
        )
        high, low = split(turned)
        spec = dot(jnp.concatenate([high, low, high], 1), second)
        out.append((spec[:, :width], spec[:, width:]))
    return out


def inverse(spectra, second, last, twist):
    cols = []
    for re, im in spectra:
        width = re.shape[1]
        high, low = split(jnp.concatenate([re, im], 1))
        rot = dot(jnp.concatenate([high, low, high], 1), second)
        re, im = rot[:, :width], rot[:, width:]
        cols.append(
            jnp.concatenate([re * twist[0] - im * twist[1], im * twist[0] + re * twist[1]], 0)
        )
    high, low = split(jnp.concatenate(cols, 1))
    return dot(last, jnp.concatenate([high, low, high], 0))


def times(a, b):
    return [(ar * br - ai * bi, ar * bi + ai * br) for (ar, ai), (br, bi) in zip(a, b)]


def times_conj(a, b):
    return [(ar * br + ai * bi, ai * br - ar * bi) for (ar, ai), (br, bi) in zip(a, b)]


def pack_tokens(landed):
    blocks, _, width = landed.shape
    wide = landed.astype(jnp.float32)
    sides = [wide[:, h * HALF : (h + 1) * HALF, :].reshape(blocks * HALF, width) for h in range(2)]
    return jnp.concatenate(sides, 1).astype(jnp.bfloat16)


def unpack_tokens(cols, blocks):
    width = cols.shape[1] // 2
    sides = [cols[:, h * width : (h + 1) * width].reshape(blocks, HALF, width) for h in range(2)]
    return jnp.concatenate(sides, 1).astype(jnp.bfloat16)


def ctx_peer(me, step):
    turn = step // 2
    side = (turn + 1) // 2
    along = 8 + side - 2 * side * ((turn + 1) % 2)
    flip = (step + 1) % 2
    return (me // 16 + flip) % 2 * 16 + (me % 16 + along) % 16


def kernel(
    scale,
    go_hbm, q_hbm, k_hbm, v_hbm, f_ref,
    first_tok_hbm, first_filt_hbm, fwd_hbm, inv_hbm, last_tok_hbm, last_lag_hbm, twist_hbm,
    gq_ref, gk_ref, gv_ref, gf_ref,
    go, q, k, v,
    first_tok, first_filt, fwd, inv, last_tok, last_lag, twist,
    g_out, m_out, g_in, m_in, f_wide, f_out, f_in,
    back_out, conv_out, back_in, conv_in, lag_out, lag_in,
    load_sem, table_sem, send_sem, recv_sem,
):
    me, dp = lax.axis_index("ctx"), lax.axis_index("dp")
    n_ctx, n_dp = g_out.shape[0], f_in.shape[0]
    loads = [
        pltpu.make_async_copy(src, dst, load_sem.at[i])
        for i, (src, dst) in enumerate([(go_hbm, go), (q_hbm, q), (k_hbm, k), (v_hbm, v)])
    ]
    for load in loads:
        load.start()
    barrier = pltpu.get_barrier_semaphore()

    def greet_ctx(step, carry):
        pl.semaphore_signal(
            barrier, inc=1, device_id=(dp, ctx_peer(me, step)), device_id_type=MESH
        )
        return carry

    def greet_dp(step, carry):
        pl.semaphore_signal(
            barrier, inc=1, device_id=((dp + step) % n_dp, me), device_id_type=MESH
        )
        return carry

    lax.fori_loop(0, n_ctx - 1, greet_ctx, 0)
    lax.fori_loop(1, n_dp, greet_dp, 0)
    tables = [
        pltpu.make_async_copy(src, dst, table_sem.at[i])
        for i, (src, dst) in enumerate(
            [
                (first_filt_hbm, first_filt),
                (twist_hbm, twist),
                (fwd_hbm, fwd),
                (first_tok_hbm, first_tok),
                (inv_hbm, inv),
                (last_tok_hbm, last_tok),
                (last_lag_hbm, last_lag),
            ]
        )
    ]
    for table in tables:
        table.start()

    def product(a, b):
        wide = a[0].astype(jnp.float32) * b[0].astype(jnp.float32)
        return wide.T.astype(jnp.bfloat16).reshape(g_out.shape)

    loads[0].wait()
    loads[1].wait()
    g_out[...] = product(go, q)
    loads[2].wait()
    loads[3].wait()
    m_out[...] = product(k, v)
    blocks, width = f_out.shape
    row = f_ref[...].astype(jnp.float32)
    for i in range(blocks):
        f_wide[pl.ds(i, 1), :] = row[:, i * width : (i + 1) * width]
    f_out[...] = f_wide[...].astype(jnp.bfloat16)
    pl.semaphore_wait(barrier, n_ctx - 1 + n_dp - 1)

    def send_ctx(src, dst, which):
        def body(step, carry):
            peer = ctx_peer(me, step)
            pltpu.make_async_remote_copy(
                src_ref=src.at[peer],
                dst_ref=dst.at[me],
                send_sem=send_sem.at[which],
                recv_sem=recv_sem.at[which],
                device_id=(dp, peer),
                device_id_type=MESH,
            ).start()
            return carry

        lax.fori_loop(0, n_ctx - 1, body, 0)
        pltpu.make_async_copy(src.at[me], dst.at[me], recv_sem.at[which]).start()

    def send_dp(pick, dst, which):
        def body(step, carry):
            peer = (dp + step) % n_dp
            pltpu.make_async_remote_copy(
                src_ref=pick(peer),
                dst_ref=dst.at[dp],
                send_sem=send_sem.at[which],
                recv_sem=recv_sem.at[which],
                device_id=(peer, me),
                device_id_type=MESH,
            ).start()
            return carry

        lax.fori_loop(1, n_dp, body, 0)
        pltpu.make_async_copy(pick(dp), dst.at[dp], recv_sem.at[which]).start()

    def landed(dst, which):
        pltpu.make_async_copy(dst, dst, recv_sem.at[which]).wait()

    def sent(dst, which):
        rest = dst.at[pl.ds(0, dst.shape[0] - 1)]
        pltpu.make_async_copy(rest, rest, send_sem.at[which]).wait()

    send_ctx(g_out, g_in, 0)
    send_dp(lambda peer: f_out, f_in, 1)
    send_ctx(m_out, m_in, 2)

    for table in tables:
        table.wait()
    landed(f_in, 1)
    filt = jnp.concatenate(
        [f_in[h * HALF : (h + 1) * HALF].reshape(HALF * blocks, width) for h in range(2)], 1
    )
    filt_spec = forward(filt, first_filt[...], fwd[...], twist)
    landed(g_in, 0)
    grad_spec = forward(pack_tokens(g_in[...]), first_tok[...], fwd[...], twist)
    back_cols = inverse(times_conj(grad_spec, filt_spec), inv[...], last_tok[...], twist)
    back_out[...] = unpack_tokens(back_cols, blocks)
    send_ctx(back_out, back_in, 3)
    landed(m_in, 2)
    mixed_spec = forward(pack_tokens(m_in[...]), first_tok[...], fwd[...], twist)
    conv_cols = inverse(times(mixed_spec, filt_spec), inv[...], last_tok[...], twist)
    conv_out[...] = unpack_tokens(conv_cols, blocks)
    send_ctx(conv_out, conv_in, 4)
    lag_cols = inverse(times_conj(grad_spec, mixed_spec), inv[...], last_lag[...], twist)
    for h in range(2):
        lag_out[h * HALF : (h + 1) * HALF] = (
            lag_cols[:, h * width : (h + 1) * width]
            .reshape(HALF, blocks, width)
            .astype(jnp.bfloat16)
        )
    send_dp(lambda peer: lag_out.at[peer], lag_in, 5)

    def rows(arrived):
        wide = arrived[...].astype(jnp.float32).reshape(n_ctx * 2 * HALF, width)
        return wide.T

    landed(back_in, 3)
    back = rows(back_in)
    gk_ref[0] = (back * v[0].astype(jnp.float32)).astype(jnp.bfloat16)
    gv_ref[0] = (back * k[0].astype(jnp.float32)).astype(jnp.bfloat16)
    landed(lag_in, 5)
    gf_ref[...] = jnp.sum(lag_in[...].astype(jnp.float32), axis=0) * scale
    landed(conv_in, 4)
    gq_ref[0] = (rows(conv_in) * go[0].astype(jnp.float32)).astype(jnp.bfloat16)
    for which, dst in enumerate([g_in, f_in, m_in, back_in, conv_in, lag_in]):
        sent(dst, which)


def per_device(grad_out, query_proj, key_proj, value_proj, filters):
    n_ctx, n_dp = lax.axis_size("ctx"), lax.axis_size("dp")
    _, width, channels = grad_out.shape
    blocks = n_ctx
    own = channels // n_ctx
    assert own == n_dp == 2 * HALF and filters.shape == (1, blocks * width)
    tables = make_tables(blocks, width)
    scale = 1.0 / math.sqrt(grad_out.shape[0] * n_dp * n_ctx * width)
    vmem = pl.BlockSpec(memory_space=pltpu.VMEM)
    hbm = pl.BlockSpec(memory_space=pl.ANY)
    bf16, f32 = jnp.bfloat16, jnp.float32
    tok = grad_out.shape
    cols = pltpu.VMEM((n_ctx, own, width), bf16)
    rows = pltpu.VMEM((n_dp, blocks, width), bf16)
    outs = pl.pallas_call(
        functools.partial(kernel, scale),
        out_shape=[
            jax.ShapeDtypeStruct(tok, bf16),
            jax.ShapeDtypeStruct(tok, bf16),
            jax.ShapeDtypeStruct(tok, bf16),
            jax.ShapeDtypeStruct((blocks, width), f32),
        ],
        in_specs=[hbm] * 4 + [vmem] + [hbm] * len(tables),
        out_specs=[vmem] * 4,
        scratch_shapes=[pltpu.VMEM(tok, bf16)] * 4
        + [pltpu.VMEM(t.shape, t.dtype) for t in tables]
        + [cols] * 4
        + [pltpu.VMEM((blocks, width), f32), pltpu.VMEM((blocks, width), bf16), rows]
        + [cols] * 4
        + [rows] * 2
        + [
            pltpu.SemaphoreType.DMA((4,)),
            pltpu.SemaphoreType.DMA((len(tables),)),
            pltpu.SemaphoreType.DMA((6,)),
            pltpu.SemaphoreType.DMA((6,)),
        ],
        compiler_params=pltpu.CompilerParams(
            collective_id=0, has_side_effects=True, vmem_limit_bytes=40 * 1024 * 1024
        ),
        name="hyena_backward",
    )(grad_out, query_proj, key_proj, value_proj, filters, *[jnp.asarray(t) for t in tables])
    return (*outs[:3], outs[3].reshape(filters.shape))


def solution(mesh):
    tokens, channels = P("dp", "ctx", None), P(("ctx", "dp"), None)
    return jax.shard_map(
        per_device,
        mesh=mesh,
        in_specs=(tokens, tokens, tokens, tokens, channels),
        out_specs=(tokens, tokens, tokens, channels),
        check_vma=False,
    )
```

profile of v0, /device:TPU:8, one launch (start us, length us, event | category | flops | bytes accessed | tf_op | source)
XLA Modules:
  0.0 59.1 jit_solution(15338473290285893308)
XLA Ops:
  0.6 0.0 copy-start
  0.6 1.1 %copy-done = bf16[256,1536]{1,0:T(8,128)(2,1)S(1)} copy-done((bf16[256,1536]{1,0:T(8,128)(2,1)S(1)}, bf16[256,1536]{1,0:T(8,128)(2,1)}, u32[]{:S(2)}) %copy-start) | copy-done | bytes 786456
  1.8 0.0 copy-start.1
  1.8 1.1 %copy-done.1 = bf16[256,1536]{1,0:T(8,128)(2,1)S(1)} copy-done((bf16[256,1536]{1,0:T(8,128)(2,1)S(1)}, bf16[256,1536]{1,0:T(8,128)(2,1)}, u32[]{:S(2)}) %copy-start.1) | copy-done | bytes 786456
  2.9 0.0 copy-start.2
  2.9 1.0 %copy-done.2 = bf16[512,512]{1,0:T(8,128)(2,1)S(1)} copy-done((bf16[512,512]{1,0:T(8,128)(2,1)S(1)}, bf16[512,512]{1,0:T(8,128)(2,1)}, u32[]{:S(2)}) %copy-start.2) | copy-done | bytes 524312
  3.9 0.0 copy-start.3
  3.9 1.0 %copy-done.3 = bf16[512,512]{1,0:T(8,128)(2,1)S(1)} copy-done((bf16[512,512]{1,0:T(8,128)(2,1)S(1)}, bf16[512,512]{1,0:T(8,128)(2,1)}, u32[]{:S(2)}) %copy-start.3) | copy-done | bytes 524312
  5.0 0.0 copy-start.4
  5.0 1.0 %copy-done.4 = bf16[768,256]{1,0:T(8,128)(2,1)S(1)} copy-done((bf16[768,256]{1,0:T(8,128)(2,1)S(1)}, bf16[768,256]{1,0:T(8,128)(2,1)}, u32[]{:S(2)}) %copy-start.4) | copy-done | bytes 393240
  6.0 0.0 copy-start.5
  6.0 1.0 %copy-done.5 = bf16[768,256]{1,0:T(8,128)(2,1)S(1)} copy-done((bf16[768,256]{1,0:T(8,128)(2,1)S(1)}, bf16[768,256]{1,0:T(8,128)(2,1)}, u32[]{:S(2)}) %copy-start.5) | copy-done | bytes 393240
  7.0 0.0 copy-start.6
  7.0 0.9 %copy-done.6 = f32[2,256,128]{2,1,0:T(8,128)S(1)} copy-done((f32[2,256,128]{2,1,0:T(8,128)S(1)}, f32[2,256,128]{2,1,0:T(8,128)}, u32[]{:S(2)}) %copy-start.6) | copy-done | bytes 262168
  7.9 0.0 copy-start.7
  7.9 0.9 %copy-done.7 = bf16[1,128,512]{2,1,0:T(8,128)(2,1)S(1)} copy-done((bf16[1,128,512]{2,1,0:T(8,128)(2,1)S(1)}, bf16[1,128,512]{2,1,0:T(8,128)(2,1)}, u32[]{:S(2)}) %copy-start.7) | copy-done | bytes 131096
  8.8 0.0 copy-start.8
  8.8 0.9 %copy-done.8 = bf16[1,128,512]{2,1,0:T(8,128)(2,1)S(1)} copy-done((bf16[1,128,512]{2,1,0:T(8,128)(2,1)S(1)}, bf16[1,128,512]{2,1,0:T(8,128)(2,1)}, u32[]{:S(2)}) %copy-start.8) | copy-done | bytes 131096
  9.7 0.0 copy-start.9
  9.7 0.9 %copy-done.9 = bf16[1,128,512]{2,1,0:T(8,128)(2,1)S(1)} copy-done((bf16[1,128,512]{2,1,0:T(8,128)(2,1)S(1)}, bf16[1,128,512]{2,1,0:T(8,128)(2,1)}, u32[]{:S(2)}) %copy-start.9) | copy-done | bytes 131096
  10.6 0.0 copy-start.10
  10.6 0.9 %copy-done.10 = bf16[1,128,512]{2,1,0:T(8,128)(2,1)S(1)} copy-done((bf16[1,128,512]{2,1,0:T(8,128)(2,1)S(1)}, bf16[1,128,512]{2,1,0:T(8,128)(2,1)}, u32[]{:S(2)}) %copy-start.10) | copy-done | bytes 131096
  11.5 0.0 copy-start.11
  11.6 0.7 %copy-done.11 = bf16[1,4096]{1,0:T(2,128)(2,1)S(1)} copy-done((bf16[1,4096]{1,0:T(2,128)(2,1)S(1)}, bf16[1,4096]{1,0:T(2,128)(2,1)}, u32[]{:S(2)}) %copy-start.11) | copy-done | bytes 8216
  12.3 44.3 %hyena_backward.1 = (bf16[1,128,512]{2,1,0:T(8,128)(2,1)S(1)}, bf16[1,128,512]{2,1,0:T(8,128)(2,1)S(1)}, bf16[1,128,512]{2,1,0:T(8,128)(2,1)S(1)}, f32[32,128]{1,0:T(8,128)S(1)}) custom-call(bf16[1,128,512]{2,1,0:T(8,128)(2,1)S(1)} %copy-done.7, bf16[1,128,512]{2,1,0:T(8,128)(2,1)S(1)} %copy-done.8, bf16[1,128,512]{2,1,0:T(8,128)(2,1)S(1)} %copy-done.9, ...), custom_call_target="tpu_custom_call" | custom-call | tf_op jit(solution)/shard_map/hyena_backward/pallas_call | solution.py:308
  56.5 0.7 %copy.20 = bf16[1,128,512]{2,1,0:T(8,128)(2,1)} copy(bf16[1,128,512]{2,1,0:T(8,128)(2,1)S(1)} %get-tuple-element.16) | data formatting | bytes 262144
  57.2 0.7 %copy.21 = bf16[1,128,512]{2,1,0:T(8,128)(2,1)} copy(bf16[1,128,512]{2,1,0:T(8,128)(2,1)S(1)} %get-tuple-element.17) | data formatting | bytes 262144
  57.8 0.7 %copy.22 = bf16[1,128,512]{2,1,0:T(8,128)(2,1)} copy(bf16[1,128,512]{2,1,0:T(8,128)(2,1)S(1)} %get-tuple-element.18) | data formatting | bytes 262144
  58.5 0.6 %copy.23 = f32[1,4096]{1,0:T(1,128)} copy(f32[1,4096]{1,0:T(1,128)S(1)} %bitcast.1) | data formatting | bytes 32768
Async XLA Ops:
  0.6 1.1 %copy-start = (bf16[256,1536]{1,0:T(8,128)(2,1)S(1)}, bf16[256,1536]{1,0:T(8,128)(2,1)}, u32[]{:S(2)}) copy-start(bf16[256,1536]{1,0:T(8,128)(2,1)} %constant.19.clone.last_lag_hbm) | copy-start | bytes 2359300
  1.8 1.1 %copy-start.1 = (bf16[256,1536]{1,0:T(8,128)(2,1)S(1)}, bf16[256,1536]{1,0:T(8,128)(2,1)}, u32[]{:S(2)}) copy-start(bf16[256,1536]{1,0:T(8,128)(2,1)} %constant.18.clone.last_tok_hbm) | copy-start | bytes 2359300
  2.9 1.0 %copy-start.2 = (bf16[512,512]{1,0:T(8,128)(2,1)S(1)}, bf16[512,512]{1,0:T(8,128)(2,1)}, u32[]{:S(2)}) copy-start(bf16[512,512]{1,0:T(8,128)(2,1)} %constant.15.clone.first_filt_hbm) | copy-start | bytes 1572868
  3.9 1.0 %copy-start.3 = (bf16[512,512]{1,0:T(8,128)(2,1)S(1)}, bf16[512,512]{1,0:T(8,128)(2,1)}, u32[]{:S(2)}) copy-start(bf16[512,512]{1,0:T(8,128)(2,1)} %constant.14.clone.first_tok_hbm) | copy-start | bytes 1572868
  5.0 1.0 %copy-start.4 = (bf16[768,256]{1,0:T(8,128)(2,1)S(1)}, bf16[768,256]{1,0:T(8,128)(2,1)}, u32[]{:S(2)}) copy-start(bf16[768,256]{1,0:T(8,128)(2,1)} %constant.17.clone.inv_hbm) | copy-start | bytes 1179652
  6.0 1.0 %copy-start.5 = (bf16[768,256]{1,0:T(8,128)(2,1)S(1)}, bf16[768,256]{1,0:T(8,128)(2,1)}, u32[]{:S(2)}) copy-start(bf16[768,256]{1,0:T(8,128)(2,1)} %constant.16.clone.fwd_hbm) | copy-start | bytes 1179652
  7.0 0.9 %copy-start.6 = (f32[2,256,128]{2,1,0:T(8,128)S(1)}, f32[2,256,128]{2,1,0:T(8,128)}, u32[]{:S(2)}) copy-start(f32[2,256,128]{2,1,0:T(8,128)} %constant.20.clone.twist_hbm) | copy-start | bytes 786436
  7.9 0.9 %copy-start.7 = (bf16[1,128,512]{2,1,0:T(8,128)(2,1)S(1)}, bf16[1,128,512]{2,1,0:T(8,128)(2,1)}, u32[]{:S(2)}) copy-start(bf16[1,128,512]{2,1,0:T(8,128)(2,1)} %go_hbm.1) | copy-start | bytes 393220
  8.8 0.9 %copy-start.8 = (bf16[1,128,512]{2,1,0:T(8,128)(2,1)S(1)}, bf16[1,128,512]{2,1,0:T(8,128)(2,1)}, u32[]{:S(2)}) copy-start(bf16[1,128,512]{2,1,0:T(8,128)(2,1)} %q_hbm.1) | copy-start | bytes 393220
  9.7 0.9 %copy-start.9 = (bf16[1,128,512]{2,1,0:T(8,128)(2,1)S(1)}, bf16[1,128,512]{2,1,0:T(8,128)(2,1)}, u32[]{:S(2)}) copy-start(bf16[1,128,512]{2,1,0:T(8,128)(2,1)} %k_hbm.1) | copy-start | bytes 393220
  10.6 0.9 %copy-start.10 = (bf16[1,128,512]{2,1,0:T(8,128)(2,1)S(1)}, bf16[1,128,512]{2,1,0:T(8,128)(2,1)}, u32[]{:S(2)}) copy-start(bf16[1,128,512]{2,1,0:T(8,128)(2,1)} %v_hbm.1) | copy-start | bytes 393220
  11.5 0.7 %copy-start.11 = (bf16[1,4096]{1,0:T(2,128)(2,1)S(1)}, bf16[1,4096]{1,0:T(2,128)(2,1)}, u32[]{:S(2)}) copy-start(bf16[1,4096]{1,0:T(2,128)(2,1)} %f_ref.1) | copy-start | bytes 24580
where the time goes:
time: 59.6 us; the launch traced here: 59.1 us
  Pallas kernels  44.3 us (74%)
  local copies, waits for them, and re-layouts  14.2 us (24%)
  between operations  0.66 us (1%)
    pallas_call x1, Pallas kernels, per_device(): pl.pallas_call(functools.partial(kernel, scale), out_shape=[jax.ShapeDtyp...  44.3 us
    unnamed x28, local copies, waits for them, and re-layouts  14.2 us

commit v1 on v0

--- a/solution.py
+++ b/solution.py
@@ -139,10 +139,10 @@
 
 def kernel(
     scale,
-    go_hbm, q_hbm, k_hbm, v_hbm, f_ref,
+    go_hbm, q_hbm, k_hbm, v_hbm, f_hbm,
     first_tok_hbm, first_filt_hbm, fwd_hbm, inv_hbm, last_tok_hbm, last_lag_hbm, twist_hbm,
-    gq_ref, gk_ref, gv_ref, gf_ref,
-    go, q, k, v,
+    gq_ref, gk_ref, gf_ref,
+    go, q, k, v, f_row,
     first_tok, first_filt, fwd, inv, last_tok, last_lag, twist,
     g_out, m_out, g_in, m_in, f_wide, f_out, f_in,
     back_out, conv_out, back_in, conv_in, lag_out, lag_in,
@@ -152,7 +152,7 @@
     n_ctx, n_dp = g_out.shape[0], f_in.shape[0]
     loads = [
         pltpu.make_async_copy(src, dst, load_sem.at[i])
-        for i, (src, dst) in enumerate([(go_hbm, go), (q_hbm, q), (k_hbm, k), (v_hbm, v)])
+        for i, (src, dst) in enumerate([(go_hbm, go), (q_hbm, q), (k_hbm, k), (v_hbm, v), (f_hbm, f_row)])
     ]
     for load in loads:
         load.start()
@@ -170,8 +170,8 @@
         )
         return carry
 
-    lax.fori_loop(0, n_ctx - 1, greet_ctx, 0)
-    lax.fori_loop(1, n_dp, greet_dp, 0)
+    lax.fori_loop(0, n_ctx - 1, greet_ctx, 0, unroll=True)
+    lax.fori_loop(1, n_dp, greet_dp, 0, unroll=True)
     tables = [
         pltpu.make_async_copy(src, dst, table_sem.at[i])
         for i, (src, dst) in enumerate(
@@ -200,7 +200,8 @@
     loads[3].wait()
     m_out[...] = product(k, v)
     blocks, width = f_out.shape
-    row = f_ref[...].astype(jnp.float32)
+    loads[4].wait()
+    row = f_row[...].astype(jnp.float32)
     for i in range(blocks):
         f_wide[pl.ds(i, 1), :] = row[:, i * width : (i + 1) * width]
     f_out[...] = f_wide[...].astype(jnp.bfloat16)
@@ -219,7 +220,7 @@
             ).start()
             return carry
 
-        lax.fori_loop(0, n_ctx - 1, body, 0)
+        lax.fori_loop(0, n_ctx - 1, body, 0, unroll=True)
         pltpu.make_async_copy(src.at[me], dst.at[me], recv_sem.at[which]).start()
 
     def send_dp(pick, dst, which):
@@ -235,7 +236,7 @@
             ).start()
             return carry
 
-        lax.fori_loop(1, n_dp, body, 0)
+        lax.fori_loop(1, n_dp, body, 0, unroll=True)
         pltpu.make_async_copy(pick(dp), dst.at[dp], recv_sem.at[which]).start()
 
     def landed(dst, which):
@@ -281,12 +282,11 @@
 
     landed(back_in, 3)
     back = rows(back_in)
-    gk_ref[0] = (back * v[0].astype(jnp.float32)).astype(jnp.bfloat16)
-    gv_ref[0] = (back * k[0].astype(jnp.float32)).astype(jnp.bfloat16)
+    gk_ref[0] = back.astype(jnp.bfloat16)
     landed(lag_in, 5)
     gf_ref[...] = jnp.sum(lag_in[...].astype(jnp.float32), axis=0) * scale
     landed(conv_in, 4)
-    gq_ref[0] = (rows(conv_in) * go[0].astype(jnp.float32)).astype(jnp.bfloat16)
+    gq_ref[0] = rows(conv_in).astype(jnp.bfloat16)
     for which, dst in enumerate([g_in, f_in, m_in, back_in, conv_in, lag_in]):
         sent(dst, which)
 
@@ -300,7 +300,7 @@
     tables = make_tables(blocks, width)
     scale = 1.0 / math.sqrt(grad_out.shape[0] * n_dp * n_ctx * width)
     vmem = pl.BlockSpec(memory_space=pltpu.VMEM)
-    hbm = pl.BlockSpec(memory_space=pl.ANY)
+    hbm = pl.BlockSpec(memory_space=pltpu.HBM)
     bf16, f32 = jnp.bfloat16, jnp.float32
     tok = grad_out.shape
     cols = pltpu.VMEM((n_ctx, own, width), bf16)
@@ -310,29 +310,31 @@
         out_shape=[
             jax.ShapeDtypeStruct(tok, bf16),
             jax.ShapeDtypeStruct(tok, bf16),
-            jax.ShapeDtypeStruct(tok, bf16),
             jax.ShapeDtypeStruct((blocks, width), f32),
         ],
-        in_specs=[hbm] * 4 + [vmem] + [hbm] * len(tables),
-        out_specs=[vmem] * 4,
+        in_specs=[hbm] * (5 + len(tables)),
+        out_specs=[vmem] * 3,
         scratch_shapes=[pltpu.VMEM(tok, bf16)] * 4
+        + [pltpu.VMEM(filters.shape, bf16)]
         + [pltpu.VMEM(t.shape, t.dtype) for t in tables]
         + [cols] * 4
         + [pltpu.VMEM((blocks, width), f32), pltpu.VMEM((blocks, width), bf16), rows]
         + [cols] * 4
         + [rows] * 2
         + [
-            pltpu.SemaphoreType.DMA((4,)),
+            pltpu.SemaphoreType.DMA((5,)),
             pltpu.SemaphoreType.DMA((len(tables),)),
             pltpu.SemaphoreType.DMA((6,)),
             pltpu.SemaphoreType.DMA((6,)),
         ],
         compiler_params=pltpu.CompilerParams(
-            collective_id=0, has_side_effects=True, vmem_limit_bytes=40 * 1024 * 1024
+            collective_id=0, has_side_effects=True, vmem_limit_bytes=63 * 1024 * 1024
         ),
         name="hyena_backward",
     )(grad_out, query_proj, key_proj, value_proj, filters, *[jnp.asarray(t) for t in tables])
-    return (*outs[:3], outs[3].reshape(filters.shape))
+    wide = lambda x: x.astype(f32)
+    conv, back = wide(outs[0]), wide(outs[1])
+    return ((conv*wide(grad_out)).astype(bf16),(back*wide(value_proj)).astype(bf16),(back*wide(key_proj)).astype(bf16), outs[2].reshape(filters.shape))
 
 
 def solution(mesh):

time: 59.6 us -> 47.3 us (0.79)
  local copies, waits for them, and re-layouts: 14.2 us -> 0.62 us
  other arithmetic: 0 us -> 1.77 us
    unnamed x28 -> x9, local copies, waits for them, and re-layouts: 14.2 us -> 0.62 us
    convert_element_type x0 -> x1, other arithmetic: none -> 1.77 us  [per_device(): (back * wide(key_proj)).astype(bf16)]
where the time goes in v1:
time: 47.3 us; the launch traced here: 47.2 us
  Pallas kernels  44.1 us (93%)
  other arithmetic  1.77 us (4%)
  between operations  0.7 us (1%)
  local copies, waits for them, and re-layouts  0.62 us (1%)
    pallas_call x1, Pallas kernels, per_device(): pl.pallas_call(functools.partial(kernel, scale), out_shape=[jax.ShapeDtyp...  44.1 us
    convert_element_type x1, other arithmetic, per_device(): (back * wide(key_proj)).astype(bf16)  1.77 us

profile of v1, /device:TPU:8, one launch (start us, length us, event | category | flops | bytes accessed | tf_op | source)
XLA Modules:
  0.0 47.2 jit_solution(12013835431080388090)
XLA Ops:
  0.6 0.0 copy-start.2
  0.6 0.0 copy-start.1
  0.7 0.0 copy-start
  0.7 44.1 %hyena_backward.1 = (bf16[1,128,512]{2,1,0:T(8,128)(2,1)}, bf16[1,128,512]{2,1,0:T(8,128)(2,1)}, f32[32,128]{1,0:T(8,128)}) custom-call(bf16[1,128,512]{2,1,0:T(8,128)(2,1)} %go_hbm.1, bf16[1,128,512]{2,1,0:T(8,128)(2,1)} %q_hbm.1, bf16[1,128,512]{2,1,0:T(8,128)(2,1)} %k_hbm.1, bf16[1,128,512]{2,1,0:T(8,128)(2,1)} %v_hbm.1, bf16[1,4096]{1,0:T(2,128)(2,1)} %f_hbm.1, ...), custom_call_target="tpu_custom_call" | custom-call | tf_op jit(solution)/shard_map/hyena_backward/pallas_call | solution.py:308
  44.8 0.0 copy-done.2
  44.8 0.0 copy-done.1
  44.8 0.0 copy-done
  44.8 0.0 copy-start.3
  44.8 1.8 %fusion.1 = (bf16[1,128,512]{2,1,0:T(8,128)(2,1)}, bf16[1,128,512]{2,1,0:T(8,128)(2,1)}, bf16[1,128,512]{2,1,0:T(8,128)(2,1)}) fusion(bf16[1,128,512]{2,1,0:T(8,128)(2,1)} %get-tuple-element.8, bf16[1,128,512]{2,1,0:T(8,128)(2,1)S(1)} %copy-done.1, bf16[1,128,512]{2,1,0:T(8,128)(2,1)S(1)} %copy-done.2, bf16[1,128,512]{2,1,0:T(8,128)(2,1)S(1)} %copy-done, ...), kind=kLoop, calls=%fused_computation.3 | loop fusion | flops 720896 | bytes 1048576 | tf_op jit(solution)/shard_map/convert_element_type | solution.py:337
  46.6 0.0 copy-done.3
  46.6 0.6 %copy.17 = f32[1,4096]{1,0:T(1,128)} copy(f32[1,4096]{1,0:T(1,128)S(1)} %bitcast.1) | data formatting | bytes 32768
Async XLA Ops:
  0.6 44.1 %copy-start.2 = (bf16[1,128,512]{2,1,0:T(8,128)(2,1)S(1)}, bf16[1,128,512]{2,1,0:T(8,128)(2,1)}, u32[]{:S(2)}) copy-start(bf16[1,128,512]{2,1,0:T(8,128)(2,1)} %v_hbm.1) | copy-start | bytes 393220
  0.6 44.1 %copy-start.1 = (bf16[1,128,512]{2,1,0:T(8,128)(2,1)S(1)}, bf16[1,128,512]{2,1,0:T(8,128)(2,1)}, u32[]{:S(2)}) copy-start(bf16[1,128,512]{2,1,0:T(8,128)(2,1)} %k_hbm.1) | copy-start | bytes 393220
  0.7 44.1 %copy-start = (bf16[1,128,512]{2,1,0:T(8,128)(2,1)S(1)}, bf16[1,128,512]{2,1,0:T(8,128)(2,1)}, u32[]{:S(2)}) copy-start(bf16[1,128,512]{2,1,0:T(8,128)(2,1)} %go_hbm.1) | copy-start | bytes 393220
  44.8 1.8 %copy-start.3 = (f32[32,128]{1,0:T(8,128)S(1)}, f32[32,128]{1,0:T(8,128)}, u32[]{:S(2)}) copy-start(f32[32,128]{1,0:T(8,128)} %get-tuple-element.9) | copy-start | bytes 49156

commit v2 on v1

--- a/solution.py
+++ b/solution.py
@@ -13,6 +13,7 @@
 MESH = pl.DeviceIdType.MESH
 BF16 = ml_dtypes.bfloat16
 HALF = 8
+ROW = 16
 
 
 def split_table(table):
@@ -129,24 +130,20 @@
     return jnp.concatenate(sides, 1).astype(jnp.bfloat16)
 
 
-def ctx_peer(me, step):
-    turn = step // 2
-    side = (turn + 1) // 2
-    along = 8 + side - 2 * side * ((turn + 1) % 2)
-    flip = (step + 1) % 2
-    return (me // 16 + flip) % 2 * 16 + (me % 16 + along) % 16
+def along(me, step):
+    side = (step + 1) // 2
+    return (me + 8 + side - 2 * side * ((step + 1) % 2)) % ROW
 
 
 def kernel(
-    scale,
     go_hbm, q_hbm, k_hbm, v_hbm, f_hbm,
     first_tok_hbm, first_filt_hbm, fwd_hbm, inv_hbm, last_tok_hbm, last_lag_hbm, twist_hbm,
-    gq_ref, gk_ref, gf_ref,
+    conv_in, back_in, lag_in,
     go, q, k, v, f_row,
     first_tok, first_filt, fwd, inv, last_tok, last_lag, twist,
     g_out, m_out, g_in, m_in, f_wide, f_out, f_in,
-    back_out, conv_out, back_in, conv_in, lag_out, lag_in,
-    load_sem, table_sem, send_sem, recv_sem,
+    back_out, conv_out, lag_out,
+    load_sem, table_sem, send_sem, recv_sem, row_sem,
 ):
     me, dp = lax.axis_index("ctx"), lax.axis_index("dp")
     n_ctx, n_dp = g_out.shape[0], f_in.shape[0]
@@ -158,20 +155,23 @@
         load.start()
     barrier = pltpu.get_barrier_semaphore()
 
-    def greet_ctx(step, carry):
-        pl.semaphore_signal(
-            barrier, inc=1, device_id=(dp, ctx_peer(me, step)), device_id_type=MESH
-        )
-        return carry
-
-    def greet_dp(step, carry):
+    row = me // ROW
+
+    def greet(sem, z, x):
+        pl.semaphore_signal(sem, inc=1, device_id=(dp, x * ROW + z), device_id_type=MESH)
+
+    for step in range(ROW - 1):
+        greet(barrier, along(me, step), row)
+
+    @pl.when(row == 0)
+    def _():
+        for step in range(ROW):
+            greet(barrier, along(me, step), 1)
+
+    for step in range(1, n_dp):
         pl.semaphore_signal(
             barrier, inc=1, device_id=((dp + step) % n_dp, me), device_id_type=MESH
         )
-        return carry
-
-    lax.fori_loop(0, n_ctx - 1, greet_ctx, 0, unroll=True)
-    lax.fori_loop(1, n_dp, greet_dp, 0, unroll=True)
     tables = [
         pltpu.make_async_copy(src, dst, table_sem.at[i])
         for i, (src, dst) in enumerate(
@@ -201,26 +201,42 @@
     m_out[...] = product(k, v)
     blocks, width = f_out.shape
     loads[4].wait()
-    row = f_row[...].astype(jnp.float32)
+    taps = f_row[...].astype(jnp.float32)
     for i in range(blocks):
-        f_wide[pl.ds(i, 1), :] = row[:, i * width : (i + 1) * width]
+        f_wide[pl.ds(i, 1), :] = taps[:, i * width : (i + 1) * width]
     f_out[...] = f_wide[...].astype(jnp.bfloat16)
-    pl.semaphore_wait(barrier, n_ctx - 1 + n_dp - 1)
-
-    def send_ctx(src, dst, which):
-        def body(step, carry):
-            peer = ctx_peer(me, step)
-            pltpu.make_async_remote_copy(
-                src_ref=src.at[peer],
-                dst_ref=dst.at[me],
-                send_sem=send_sem.at[which],
-                recv_sem=recv_sem.at[which],
-                device_id=(dp, peer),
-                device_id_type=MESH,
-            ).start()
-            return carry
-
-        lax.fori_loop(0, n_ctx - 1, body, 0, unroll=True)
+    pl.semaphore_wait(barrier, ROW - 1 + n_dp - 1 + ROW * row)
+
+    @pl.when(row == 1)
+    def _():
+        greet(row_sem, me % ROW, 0)
+
+    def send_one(src, dst, which, to, z):
+        peer = to * ROW + z
+        pltpu.make_async_remote_copy(
+            src_ref=src.at[peer],
+            dst_ref=dst.at[me],
+            send_sem=send_sem.at[which],
+            recv_sem=recv_sem.at[which],
+            device_id=(dp, peer),
+            device_id_type=MESH,
+        ).start()
+
+    def send_same(src, dst, which):
+        for step in range(ROW - 1):
+            send_one(src, dst, which, row, along(me, step))
+
+    def send_cross(src, dst, which):
+        for step in range(ROW):
+            send_one(src, dst, which, 1 - row, along(me, step))
+
+    def send_both(src, dst, which, first=1):
+        for step in range(ROW):
+            for flip in (first, 1 - first):
+                if flip or step < ROW - 1:
+                    send_one(src, dst, which, (row + flip) % 2, along(me, step))
+
+    def keep(src, dst, which):
         pltpu.make_async_copy(src.at[me], dst.at[me], recv_sem.at[which]).start()
 
     def send_dp(pick, dst, which):
@@ -246,10 +262,22 @@
         rest = dst.at[pl.ds(0, dst.shape[0] - 1)]
         pltpu.make_async_copy(rest, rest, send_sem.at[which]).wait()
 
-    send_ctx(g_out, g_in, 0)
+    keep(g_out, g_in, 0)
+    keep(m_out, m_in, 2)
+
+    @pl.when(row == 0)
+    def _():
+        send_same(g_out, g_in, 0)
+        pl.semaphore_wait(row_sem, 1)
+        send_cross(g_out, g_in, 0)
+        send_both(m_out, m_in, 2)
+
+    @pl.when(row == 1)
+    def _():
+        send_both(g_out, g_in, 0)
+        send_both(m_out, m_in, 2)
+
     send_dp(lambda peer: f_out, f_in, 1)
-    send_ctx(m_out, m_in, 2)
-
     for table in tables:
         table.wait()
     landed(f_in, 1)
@@ -261,12 +289,22 @@
     grad_spec = forward(pack_tokens(g_in[...]), first_tok[...], fwd[...], twist)
     back_cols = inverse(times_conj(grad_spec, filt_spec), inv[...], last_tok[...], twist)
     back_out[...] = unpack_tokens(back_cols, blocks)
-    send_ctx(back_out, back_in, 3)
+    keep(back_out, back_in, 3)
+    send_both(back_out, back_in, 3)
     landed(m_in, 2)
     mixed_spec = forward(pack_tokens(m_in[...]), first_tok[...], fwd[...], twist)
     conv_cols = inverse(times(mixed_spec, filt_spec), inv[...], last_tok[...], twist)
     conv_out[...] = unpack_tokens(conv_cols, blocks)
-    send_ctx(conv_out, conv_in, 4)
+    keep(conv_out, conv_in, 4)
+
+    @pl.when(row == 0)
+    def _():
+        send_both(conv_out, conv_in, 4)
+
+    @pl.when(row == 1)
+    def _():
+        send_cross(conv_out, conv_in, 4)
+        send_same(conv_out, conv_in, 4)
     lag_cols = inverse(times_conj(grad_spec, mixed_spec), inv[...], last_lag[...], twist)
     for h in range(2):
         lag_out[h * HALF : (h + 1) * HALF] = (
@@ -276,19 +314,24 @@
         )
     send_dp(lambda peer: lag_out.at[peer], lag_in, 5)
 
-    def rows(arrived):
-        wide = arrived[...].astype(jnp.float32).reshape(n_ctx * 2 * HALF, width)
-        return wide.T
-
     landed(back_in, 3)
-    back = rows(back_in)
-    gk_ref[0] = back.astype(jnp.bfloat16)
     landed(lag_in, 5)
-    gf_ref[...] = jnp.sum(lag_in[...].astype(jnp.float32), axis=0) * scale
     landed(conv_in, 4)
-    gq_ref[0] = rows(conv_in).astype(jnp.bfloat16)
     for which, dst in enumerate([g_in, f_in, m_in, back_in, conv_in, lag_in]):
         sent(dst, which)
+
+
+def gate(scale, conv, back, lag, go, k, v, gq_ref, gk_ref, gv_ref, gf_ref):
+    channels, width = go.shape[2], go.shape[1]
+
+    def rows(arrived):
+        return arrived[...].astype(jnp.float32).reshape(channels, width).T
+
+    cols = rows(back)
+    gk_ref[0] = (cols * v[0].astype(jnp.float32)).astype(jnp.bfloat16)
+    gv_ref[0] = (cols * k[0].astype(jnp.float32)).astype(jnp.bfloat16)
+    gq_ref[0] = (rows(conv) * go[0].astype(jnp.float32)).astype(jnp.bfloat16)
+    gf_ref[...] = jnp.sum(lag[...].astype(jnp.float32), axis=0) * scale
 
 
 def per_device(grad_out, query_proj, key_proj, value_proj, filters):
@@ -306,35 +349,43 @@
     cols = pltpu.VMEM((n_ctx, own, width), bf16)
     rows = pltpu.VMEM((n_dp, blocks, width), bf16)
     outs = pl.pallas_call(
-        functools.partial(kernel, scale),
+        kernel,
         out_shape=[
-            jax.ShapeDtypeStruct(tok, bf16),
-            jax.ShapeDtypeStruct(tok, bf16),
-            jax.ShapeDtypeStruct((blocks, width), f32),
+            jax.ShapeDtypeStruct((n_ctx, own, width), bf16),
+            jax.ShapeDtypeStruct((n_ctx, own, width), bf16),
+            jax.ShapeDtypeStruct((n_dp, blocks, width), bf16),
         ],
         in_specs=[hbm] * (5 + len(tables)),
-        out_specs=[vmem] * 3,
+        out_specs=[hbm] * 3,
         scratch_shapes=[pltpu.VMEM(tok, bf16)] * 4
         + [pltpu.VMEM(filters.shape, bf16)]
         + [pltpu.VMEM(t.shape, t.dtype) for t in tables]
         + [cols] * 4
         + [pltpu.VMEM((blocks, width), f32), pltpu.VMEM((blocks, width), bf16), rows]
-        + [cols] * 4
-        + [rows] * 2
+        + [cols] * 2
+        + [rows]
         + [
             pltpu.SemaphoreType.DMA((5,)),
             pltpu.SemaphoreType.DMA((len(tables),)),
             pltpu.SemaphoreType.DMA((6,)),
             pltpu.SemaphoreType.DMA((6,)),
+            pltpu.SemaphoreType.REGULAR,
         ],
         compiler_params=pltpu.CompilerParams(
             collective_id=0, has_side_effects=True, vmem_limit_bytes=63 * 1024 * 1024
         ),
         name="hyena_backward",
     )(grad_out, query_proj, key_proj, value_proj, filters, *[jnp.asarray(t) for t in tables])
-    wide = lambda x: x.astype(f32)
-    conv, back = wide(outs[0]), wide(outs[1])
-    return ((conv*wide(grad_out)).astype(bf16),(back*wide(value_proj)).astype(bf16),(back*wide(key_proj)).astype(bf16), outs[2].reshape(filters.shape))
+    outs = pl.pallas_call(
+        functools.partial(gate, scale),
+        out_shape=[jax.ShapeDtypeStruct(tok, bf16)] * 3
+        + [jax.ShapeDtypeStruct((blocks, width), f32)],
+        in_specs=[vmem] * 6,
+        out_specs=[vmem] * 4,
+        compiler_params=pltpu.CompilerParams(vmem_limit_bytes=63 * 1024 * 1024),
+        name="gate_outputs",
+    )(outs[0], outs[1], outs[2], grad_out, key_proj, value_proj)
+    return (*outs[:3], outs[3].reshape(filters.shape))
 
 
 def solution(mesh):

time: 47.3 us -> 45.2 us (0.956)
  the two profiles are of different devices: /device:TPU:8 before, /device:TPU:30 now
where the time goes in v2:
time: 45.2 us; the launch traced here: 45.1 us
  Pallas kernels  44.4 us (98%)
  between operations  0.64 us (1%)
    pallas_call x1, Pallas kernels, per_device(): pl.pallas_call(kernel, out_shape=[jax.ShapeDtypeStruct((n_ctx, own, width...  42.4 us
    pallas_call x1, Pallas kernels, per_device(): pl.pallas_call(functools.partial(gate, scale), out_shape=[jax.ShapeDtypeS...  2.08 us

profile of v2, /device:TPU:30, one launch (start us, length us, event | category | flops | bytes accessed | tf_op | source)
XLA Modules:
  0.0 45.1 jit_solution(12845992943288133664)
XLA Ops:
  0.6 42.4 %hyena_backward.1 = (bf16[32,16,128]{2,1,0:T(8,128)(2,1)}, bf16[32,16,128]{2,1,0:T(8,128)(2,1)}, bf16[16,32,128]{2,1,0:T(8,128)(2,1)}) custom-call(bf16[1,128,512]{2,1,0:T(8,128)(2,1)} %go.1, bf16[1,128,512]{2,1,0:T(8,128)(2,1)} %q_hbm.1, bf16[1,128,512]{2,1,0:T(8,128)(2,1)} %k.1, bf16[1,128,512]{2,1,0:T(8,128)(2,1)} %v.1, bf16[1,4096]{1,0:T(2,128)(2,1)} %f_hbm.1, ...), custom_call_target="tpu_custom_call" | custom-call | tf_op jit(solution)/shard_map/hyena_backward/pallas_call | solution.py:351
  43.0 2.1 %gate_outputs.1 = (bf16[1,128,512]{2,1,0:T(8,128)(2,1)}, bf16[1,128,512]{2,1,0:T(8,128)(2,1)}, bf16[1,128,512]{2,1,0:T(8,128)(2,1)}, f32[32,128]{1,0:T(8,128)}) custom-call(bf16[32,16,128]{2,1,0:T(8,128)(2,1)} %get-tuple-element.11.conv, bf16[32,16,128]{2,1,0:T(8,128)(2,1)} %get-tuple-element.12.back, bf16[16,32,128]{2,1,0:T(8,128)(2,1)} %get-tuple-element.13.lag, ...), custom_call_target="tpu_custom_call" | custom-call | tf_op jit(solution)/shard_map/gate_outputs/pallas_call | solution.py:379

commit v3 on v2

--- a/solution.py
+++ b/solution.py
@@ -163,11 +163,6 @@
     for step in range(ROW - 1):
         greet(barrier, along(me, step), row)
 
-    @pl.when(row == 0)
-    def _():
-        for step in range(ROW):
-            greet(barrier, along(me, step), 1)
-
     for step in range(1, n_dp):
         pl.semaphore_signal(
             barrier, inc=1, device_id=((dp + step) % n_dp, me), device_id_type=MESH
@@ -205,7 +200,11 @@
     for i in range(blocks):
         f_wide[pl.ds(i, 1), :] = taps[:, i * width : (i + 1) * width]
     f_out[...] = f_wide[...].astype(jnp.bfloat16)
-    pl.semaphore_wait(barrier, ROW - 1 + n_dp - 1 + ROW * row)
+    pl.semaphore_wait(barrier, ROW - 1 + n_dp - 1 + row)
+
+    @pl.when(row == 0)
+    def _():
+        greet(barrier, me % ROW, 1)
 
     @pl.when(row == 1)
     def _():
@@ -274,7 +273,8 @@
 
     @pl.when(row == 1)
     def _():
-        send_both(g_out, g_in, 0)
+        send_cross(g_out, g_in, 0)
+        send_same(g_out, g_in, 0)
         send_both(m_out, m_in, 2)
 
     send_dp(lambda peer: f_out, f_in, 1)

time: 45.2 us -> 45 us (level)
  the two profiles are of different devices: /device:TPU:30 before, /device:TPU:8 now
where the time goes in v3:
time: 45 us; the launch traced here: 44.9 us
  Pallas kernels  44.2 us (98%)
  between operations  0.64 us (1%)
    pallas_call x1, Pallas kernels, per_device(): pl.pallas_call(kernel, out_shape=[jax.ShapeDtypeStruct((n_ctx, own, width...  42.2 us
    pallas_call x1, Pallas kernels, per_device(): pl.pallas_call(functools.partial(gate, scale), out_shape=[jax.ShapeDtypeS...  2.08 us

profile of v3, /device:TPU:8, one launch (start us, length us, event | category | flops | bytes accessed | tf_op | source)
XLA Modules:
  0.0 44.9 jit_solution(18316484567060595222)
XLA Ops:
  0.6 42.2 %hyena_backward.1 = (bf16[32,16,128]{2,1,0:T(8,128)(2,1)}, bf16[32,16,128]{2,1,0:T(8,128)(2,1)}, bf16[16,32,128]{2,1,0:T(8,128)(2,1)}) custom-call(bf16[1,128,512]{2,1,0:T(8,128)(2,1)} %go.1, bf16[1,128,512]{2,1,0:T(8,128)(2,1)} %q_hbm.1, bf16[1,128,512]{2,1,0:T(8,128)(2,1)} %k.1, bf16[1,128,512]{2,1,0:T(8,128)(2,1)} %v.1, bf16[1,4096]{1,0:T(2,128)(2,1)} %f_hbm.1, ...), custom_call_target="tpu_custom_call" | custom-call | tf_op jit(solution)/shard_map/hyena_backward/pallas_call | solution.py:351
  42.8 2.1 %gate_outputs.1 = (bf16[1,128,512]{2,1,0:T(8,128)(2,1)}, bf16[1,128,512]{2,1,0:T(8,128)(2,1)}, bf16[1,128,512]{2,1,0:T(8,128)(2,1)}, f32[32,128]{1,0:T(8,128)}) custom-call(bf16[32,16,128]{2,1,0:T(8,128)(2,1)} %get-tuple-element.11.conv, bf16[32,16,128]{2,1,0:T(8,128)(2,1)} %get-tuple-element.12.back, bf16[16,32,128]{2,1,0:T(8,128)(2,1)} %get-tuple-element.13.lag, ...), custom_call_target="tpu_custom_call" | custom-call | tf_op jit(solution)/shard_map/gate_outputs/pallas_call | solution.py:379

commit v4 on v3

--- a/solution.py
+++ b/solution.py
@@ -151,8 +151,6 @@
         pltpu.make_async_copy(src, dst, load_sem.at[i])
         for i, (src, dst) in enumerate([(go_hbm, go), (q_hbm, q), (k_hbm, k), (v_hbm, v), (f_hbm, f_row)])
     ]
-    for load in loads:
-        load.start()
     barrier = pltpu.get_barrier_semaphore()
 
     row = me // ROW
@@ -167,6 +165,8 @@
         pl.semaphore_signal(
             barrier, inc=1, device_id=((dp + step) % n_dp, me), device_id_type=MESH
         )
+    for load in loads:
+        load.start()
     tables = [
         pltpu.make_async_copy(src, dst, table_sem.at[i])
         for i, (src, dst) in enumerate(
@@ -191,15 +191,7 @@
     loads[0].wait()
     loads[1].wait()
     g_out[...] = product(go, q)
-    loads[2].wait()
-    loads[3].wait()
-    m_out[...] = product(k, v)
     blocks, width = f_out.shape
-    loads[4].wait()
-    taps = f_row[...].astype(jnp.float32)
-    for i in range(blocks):
-        f_wide[pl.ds(i, 1), :] = taps[:, i * width : (i + 1) * width]
-    f_out[...] = f_wide[...].astype(jnp.bfloat16)
     pl.semaphore_wait(barrier, ROW - 1 + n_dp - 1 + row)
 
     @pl.when(row == 0)
@@ -262,21 +254,28 @@
         pltpu.make_async_copy(rest, rest, send_sem.at[which]).wait()
 
     keep(g_out, g_in, 0)
-    keep(m_out, m_in, 2)
 
     @pl.when(row == 0)
     def _():
         send_same(g_out, g_in, 0)
         pl.semaphore_wait(row_sem, 1)
         send_cross(g_out, g_in, 0)
-        send_both(m_out, m_in, 2)
 
     @pl.when(row == 1)
     def _():
         send_cross(g_out, g_in, 0)
         send_same(g_out, g_in, 0)
-        send_both(m_out, m_in, 2)
-
+
+    loads[2].wait()
+    loads[3].wait()
+    m_out[...] = product(k, v)
+    keep(m_out, m_in, 2)
+    send_both(m_out, m_in, 2)
+    loads[4].wait()
+    taps = f_row[...].astype(jnp.float32)
+    for i in range(blocks):
+        f_wide[pl.ds(i, 1), :] = taps[:, i * width : (i + 1) * width]
+    f_out[...] = f_wide[...].astype(jnp.bfloat16)
     send_dp(lambda peer: f_out, f_in, 1)
     for table in tables:
         table.wait()

time: 45 us -> 45.1 us (level)
  no operation moved by 1% of the time
where the time goes in v4:
time: 45.1 us; the launch traced here: 44.9 us
  Pallas kernels  44.2 us (98%)
  between operations  0.64 us (1%)
    pallas_call x1, Pallas kernels, per_device(): pl.pallas_call(kernel, out_shape=[jax.ShapeDtypeStruct((n_ctx, own, width...  42.2 us
    pallas_call x1, Pallas kernels, per_device(): pl.pallas_call(functools.partial(gate, scale), out_shape=[jax.ShapeDtypeS...  2.08 us

profile of v4, /device:TPU:8, one launch (start us, length us, event | category | flops | bytes accessed | tf_op | source)
XLA Modules:
  0.0 44.9 jit_solution(10599414253938991926)
XLA Ops:
  0.6 42.2 %hyena_backward.1 = (bf16[32,16,128]{2,1,0:T(8,128)(2,1)}, bf16[32,16,128]{2,1,0:T(8,128)(2,1)}, bf16[16,32,128]{2,1,0:T(8,128)(2,1)}) custom-call(bf16[1,128,512]{2,1,0:T(8,128)(2,1)} %go.1, bf16[1,128,512]{2,1,0:T(8,128)(2,1)} %q_hbm.1, bf16[1,128,512]{2,1,0:T(8,128)(2,1)} %k.1, bf16[1,128,512]{2,1,0:T(8,128)(2,1)} %v.1, bf16[1,4096]{1,0:T(2,128)(2,1)} %f_hbm.1, ...), custom_call_target="tpu_custom_call" | custom-call | tf_op jit(solution)/shard_map/hyena_backward/pallas_call | solution.py:350
  42.8 2.1 %gate_outputs.1 = (bf16[1,128,512]{2,1,0:T(8,128)(2,1)}, bf16[1,128,512]{2,1,0:T(8,128)(2,1)}, bf16[1,128,512]{2,1,0:T(8,128)(2,1)}, f32[32,128]{1,0:T(8,128)}) custom-call(bf16[32,16,128]{2,1,0:T(8,128)(2,1)} %get-tuple-element.11.conv, bf16[32,16,128]{2,1,0:T(8,128)(2,1)} %get-tuple-element.12.back, bf16[16,32,128]{2,1,0:T(8,128)(2,1)} %get-tuple-element.13.lag, ...), custom_call_target="tpu_custom_call" | custom-call | tf_op jit(solution)/shard_map/gate_outputs/pallas_call | solution.py:378

commit v5 on v4

--- a/solution.py
+++ b/solution.py
@@ -320,17 +320,47 @@
         sent(dst, which)
 
 
-def gate(scale, conv, back, lag, go, k, v, gq_ref, gk_ref, gv_ref, gf_ref):
+def gate(
+    scale,
+    conv_hbm, back_hbm, lag_hbm, go_hbm, k_hbm, v_hbm,
+    gq_hbm, gk_hbm, gv_hbm, gf_hbm,
+    conv, back, lag, go, k, v, gq, gk, gv, gf,
+    load_sem, store_sem,
+):
+    loads = [
+        pltpu.make_async_copy(src, dst, load_sem.at[i])
+        for i, (src, dst) in enumerate(
+            [(back_hbm, back), (v_hbm, v), (k_hbm, k), (conv_hbm, conv), (go_hbm, go), (lag_hbm, lag)]
+        )
+    ]
+    stores = [
+        pltpu.make_async_copy(src, dst, store_sem.at[i])
+        for i, (src, dst) in enumerate([(gk, gk_hbm), (gv, gv_hbm), (gq, gq_hbm), (gf, gf_hbm)])
+    ]
+    for load in loads:
+        load.start()
     channels, width = go.shape[2], go.shape[1]
 
     def rows(arrived):
         return arrived[...].astype(jnp.float32).reshape(channels, width).T
 
+    loads[0].wait()
     cols = rows(back)
-    gk_ref[0] = (cols * v[0].astype(jnp.float32)).astype(jnp.bfloat16)
-    gv_ref[0] = (cols * k[0].astype(jnp.float32)).astype(jnp.bfloat16)
-    gq_ref[0] = (rows(conv) * go[0].astype(jnp.float32)).astype(jnp.bfloat16)
-    gf_ref[...] = jnp.sum(lag[...].astype(jnp.float32), axis=0) * scale
+    loads[1].wait()
+    gk[0] = (cols * v[0].astype(jnp.float32)).astype(jnp.bfloat16)
+    stores[0].start()
+    loads[2].wait()
+    gv[0] = (cols * k[0].astype(jnp.float32)).astype(jnp.bfloat16)
+    stores[1].start()
+    loads[3].wait()
+    loads[4].wait()
+    gq[0] = (rows(conv) * go[0].astype(jnp.float32)).astype(jnp.bfloat16)
+    stores[2].start()
+    loads[5].wait()
+    gf[...] = jnp.sum(lag[...].astype(jnp.float32), axis=0) * scale
+    stores[3].start()
+    for done in stores:
+        done.wait()
 
 
 def per_device(grad_out, query_proj, key_proj, value_proj, filters):
@@ -379,8 +409,15 @@
         functools.partial(gate, scale),
         out_shape=[jax.ShapeDtypeStruct(tok, bf16)] * 3
         + [jax.ShapeDtypeStruct((blocks, width), f32)],
-        in_specs=[vmem] * 6,
-        out_specs=[vmem] * 4,
+        in_specs=[hbm] * 6,
+        out_specs=[hbm] * 4,
+        scratch_shapes=[cols, cols, rows]
+        + [pltpu.VMEM(tok, bf16)] * 6
+        + [
+            pltpu.VMEM((blocks, width), f32),
+            pltpu.SemaphoreType.DMA((6,)),
+            pltpu.SemaphoreType.DMA((4,)),
+        ],
         compiler_params=pltpu.CompilerParams(vmem_limit_bytes=63 * 1024 * 1024),
         name="gate_outputs",
     )(outs[0], outs[1], outs[2], grad_out, key_proj, value_proj)

time: 45.1 us -> 45 us (level)
  the two profiles are of different devices: /device:TPU:8 before, /device:TPU:6 now
where the time goes in v5:
time: 45 us; the launch traced here: 44.9 us
  Pallas kernels  44.3 us (98%)
  between operations  0.64 us (1%)
    pallas_call x1, Pallas kernels, per_device(): pl.pallas_call(kernel, out_shape=[jax.ShapeDtypeStruct((n_ctx, own, width...  42.2 us
    pallas_call x1, Pallas kernels, per_device(): pl.pallas_call(functools.partial(gate, scale), out_shape=[jax.ShapeDtypeS...  2.02 us

profile of v5, /device:TPU:6, one launch (start us, length us, event | category | flops | bytes accessed | tf_op | source)
XLA Modules:
  0.0 44.9 jit_solution(16365122056664592639)
XLA Ops:
  0.6 42.2 %hyena_backward.1 = (bf16[32,16,128]{2,1,0:T(8,128)(2,1)}, bf16[32,16,128]{2,1,0:T(8,128)(2,1)}, bf16[16,32,128]{2,1,0:T(8,128)(2,1)}) custom-call(bf16[1,128,512]{2,1,0:T(8,128)(2,1)} %go_hbm.3, bf16[1,128,512]{2,1,0:T(8,128)(2,1)} %q_hbm.1, bf16[1,128,512]{2,1,0:T(8,128)(2,1)} %k_hbm.3, bf16[1,128,512]{2,1,0:T(8,128)(2,1)} %v_hbm.3, ...), custom_call_target="tpu_custom_call" | custom-call | tf_op jit(solution)/shard_map/hyena_backward/pallas_call | solution.py:380
  42.9 2.0 %gate_outputs.1 = (bf16[1,128,512]{2,1,0:T(8,128)(2,1)}, bf16[1,128,512]{2,1,0:T(8,128)(2,1)}, bf16[1,128,512]{2,1,0:T(8,128)(2,1)}, f32[32,128]{1,0:T(8,128)}) custom-call(bf16[32,16,128]{2,1,0:T(8,128)(2,1)} %get-tuple-element.11.conv_hbm, bf16[32,16,128]{2,1,0:T(8,128)(2,1)} %get-tuple-element.12.back_hbm, ...), custom_call_target="tpu_custom_call" | custom-call | tf_op jit(solution)/shard_map/gate_outputs/pallas_call | solution.py:408
